TPU v7x, 256 devices: a whole 4x4x8 slice. The times are simulated.
256 devices in a mesh: dp: 16 (over x, y), tensor: 16 (over z, core).
Axes of the slice: x: 4, y: 4, z: 8, core: 2. Of those that a mesh axis runs over, the one named last changes fastest.
Arguments:
- acts: bfloat16 [32, 512, 16384], P('dp', None, 'tensor'), may hold values from -6 to 6
- grads: bfloat16 [32, 512, 53248], P('dp', None, 'tensor'), may hold values from -6 to 6
- proj_in: bfloat16 [16384, 64], P('tensor'), may hold values from -0.046875 to 0.046875
- proj_out: bfloat16 [53248, 64], P('tensor'), may hold values from -0.02734375 to 0.02734375
- lengths: int32 [32], P('dp'), may hold values from 64 to 512, as said below
- queries: int32 [16], replicated, may hold values from 0 to 31, as said below
Outputs:
- blocks: float32 [32, 4096], P('dp', 'tensor')
- scores: float32 [32, 16], P('dp')
Inputs may be any that keep to these rules, and one draw needn't show every extreme that they name: `lengths`: some example has exactly 512 tokens in use and some exactly 64. `queries`: all distinct; 0 and 31 are among them.
All inputs are finite; a program needn't handle non-finite values.
Results may differ from a plain program's by a relative error of at most 0.0003.
Values sent between devices are 32-bit elements; how exact they have to be, the bound alone decides.
No kernel may reach another device: no remote copies, remote signals or barrier semaphores. Data moves between devices by JAX's collectives and lax.ppermute only.
A program may use at most 64 MiB of HBM per device.

v0:
```python
import jax
import jax.numpy as jnp
from jax import lax
from jax.sharding import PartitionSpec as P


def body(acts, grads, proj_in, proj_out, lengths, queries):
    highest = lax.Precision.HIGHEST
    examples, seq, width_in = acts.shape
    width_out = grads.shape[2]
    rank = proj_in.shape[1]
    total_rows = examples * seq
    scale = seq ** (-0.5)
    act_rows = acts.reshape(total_rows, width_in)
    grad_rows = grads.reshape(total_rows, width_out)
    shards = lax.axis_size("tensor")
    columns = rank * rank // shards
    out_part = jnp.dot(grad_rows, proj_out, preferred_element_type=jnp.float32)
    in_part = jnp.dot(act_rows, proj_in, preferred_element_type=jnp.float32)
    summed = lax.psum(jnp.concatenate([out_part, in_part], axis=1), "tensor")
    keep = (jnp.arange(seq, dtype=jnp.int32)[None, :] < lengths[:, None]).astype(jnp.float32)
    out_rows = summed[:, :rank].reshape(examples, seq, rank) * keep[:, :, None]
    in_rows = summed[:, rank:].reshape(examples, seq, rank)
    full_blocks = jnp.einsum("esi,esj->eij", out_rows, in_rows, precision=highest) * scale
    full_blocks = full_blocks.reshape(examples, rank * rank)
    own_blocks = lax.dynamic_slice_in_dim(
        full_blocks, lax.axis_index("tensor") * columns, columns, 1
    )
    piece = lax.all_gather(full_blocks, "dp", axis=0, tiled=True)
    ids = jnp.arange(piece.shape[0], dtype=jnp.int32)
    select = (queries[:, None] == ids[None, :]).astype(jnp.float32)
    chosen = jnp.dot(select, piece, precision=highest)
    scores = jnp.dot(full_blocks, chosen.T, precision=highest) / rank
    return (own_blocks, scores)


def solution(mesh):
    return jax.shard_map(
        body,
        mesh=mesh,
        in_specs=(
            P("dp", None, "tensor"),
            P("dp", None, "tensor"),
            P("tensor", None),
            P("tensor", None),
            P("dp"),
            P(),
        ),
        out_specs=(P("dp", "tensor"), P("dp", None)),
        check_vma=False,
    )
```

profile of v0, /device:TPU:2, one launch (start us, length us, event | category | flops | bytes accessed | tf_op | source)
XLA Modules:
  0.0 163.6 jit_solution(362226926997445474)
XLA Ops:
  7.2 0.0 copy-start
  7.2 0.0 copy-start.1
  7.2 0.0 all-reduce.2.cloned.1.call-start
  7.2 1.5 copy-done
  8.8 1.7 %fusion.8 = f32[1024,64]{0,1:T(8,128)S(1)} fusion(bf16[1024,1024]{1,0:T(8,128)(2,1)S(1)} %bitcast.17, bf16[1024,64]{0,1:T(8,128)(2,1)} %param.8), kind=kOutput, calls=%fused_computation.15 | convolution fusion | flops 134217728 | bytes 2490368 | tf_op jit(solution)/shard_map/dot_general | solution.py:19
  10.4 0.0 copy-start.2
  10.4 5.2 %fusion.7 = f32[1024,64]{0,1:T(8,128)S(1)} fusion(bf16[1024,3328]{1,0:T(8,128)(2,1)} %bitcast.18, bf16[3328,64]{0,1:T(8,128)(2,1)} %param.9), kind=kOutput, calls=%fused_computation.14 | convolution fusion | flops 436207616 | bytes 7503872 | tf_op jit(solution)/shard_map/dot_general | solution.py:18
  15.6 0.8 pad_maximum_fusion
  16.4 0.0 all-reduce.2.cloned.1.call-update
  16.5 0.0 copy-done.1
  16.5 0.1 compare_convert_fusion
  16.5 112.7 %all-reduce.2.cloned.1.call-done = f32[1024,128]{0,1:T(8,128)} async-done(((f32[1024,128]{0,1:T(8,128)}), f32[1024,128]{0,1:T(8,128)}) %all-reduce.2.cloned.1.call-update) | async-done | bytes 524304 | tf_op jit(solution)/shard_map/psum | solution.py:20
  129.2 1.1 fusion.6
  130.3 0.4 convolution_multiply_fusion
  130.7 0.1 reshape.46
  130.8 0.1 reshape.47
  130.9 23.7 %all-gather = f32[16,2,4096]{2,1,0:T(2,128)S(1)} all-gather(f32[1,2,4096]{2,1,0:T(2,128)S(1)} %reshape.47), channel_id=1, replica_groups=mesh['dp'=16,'tensor'=16] {'dp'}, dimensions={0}, use_global_device_ids=true | all-gather | bytes 557056 | tf_op jit(solution)/shard_map/all_gather | solution.py:29
  154.5 0.4 reshape.48
  154.9 0.6 constant_dynamic-slice_fusion
  155.5 0.0 copy-done.2
  155.5 0.3 fusion.4
  155.8 1.0 convolution_multiply_fusion.1
Async XLA Ops:
  7.2 1.6 copy-start
  7.2 9.3 %copy-start.1 = (s32[2]{0:T(128)S(1)}, s32[2]{0:T(128)}, u32[]{:S(2)}) copy-start(s32[2]{0:T(128)} %param.10) | copy-start | bytes 28
  7.2 122.0 %all-reduce.2.cloned.1.call-start = ((), (), s32[]{:S(2)}) async-start(), calls=%async_computation | async-start | bytes 1048576 | tf_op jit(solution)/shard_map/psum | solution.py:20
  10.4 145.0 %copy-start.2 = (s32[16]{0:T(128)S(1)}, s32[16]{0:T(128)}, u32[]{:S(2)}) copy-start(s32[16]{0:T(128)} %param.11) | copy-start | bytes 196
Sparse Core Ops, SparseCore 0:
  16.6 112.5 all-reduce.1
where the time goes:
time: 164 us
  waiting for transfers between devices  113 us (69%)
  blocking collectives  23.7 us (14%)
  between operations  14.1 us (9%)
  matrix products  8.5 us (5%)
  local copies, waits for them, and re-layouts  3.74 us (2%)
    psum x1, waiting for transfers between devices, body(): summed = lax.psum(jnp.concatenate([out_part, in_part], axis=1), 'tensor')  113 us
    all_gather x1, blocking collectives, body(): piece = lax.all_gather(full_blocks, 'dp', axis=0, tiled=True)  23.7 us
    dot_general x1, matrix products, body(): out_part = jnp.dot(grad_rows, proj_out, preferred_element_type=jnp.float32)  5.16 us
  transfers between devices with their start and end apart: 1, of which 1 were waited for; matrix products, arithmetic and copies ran while one was open for 0% of the time, Pallas kernels for 0%

commit v1 on v0

--- a/solution.py
+++ b/solution.py
@@ -17,7 +17,7 @@
     columns = rank * rank // shards
     out_part = jnp.dot(grad_rows, proj_out, preferred_element_type=jnp.float32)
     in_part = jnp.dot(act_rows, proj_in, preferred_element_type=jnp.float32)
-    summed = lax.psum(jnp.concatenate([out_part, in_part], axis=1), "tensor")
+    summed = jnp.sum(lax.all_gather(jnp.concatenate([out_part, in_part], axis=1), "tensor"), axis=0)
     keep = (jnp.arange(seq, dtype=jnp.int32)[None, :] < lengths[:, None]).astype(jnp.float32)
     out_rows = summed[:, :rank].reshape(examples, seq, rank) * keep[:, :, None]
     in_rows = summed[:, rank:].reshape(examples, seq, rank)

time: 164 us -> 121 us (0.74)
  waiting for transfers between devices: 113 us -> 58.9 us
  local copies, waits for them, and re-layouts: 3.74 us -> 12.8 us
  other arithmetic: 0.91 us -> 2.89 us
    psum x1 -> x0, waiting for transfers between devices: 113 us -> none  [body(): summed = lax.psum(jnp.concatenate([out_part, in_part], axis=1), 'tensor')]
    all_gather x0 -> x1, waiting for transfers between devices: none -> 58.9 us  [body(): lax.all_gather(jnp.concatenate([out_part, in_part], axis=1), 'tensor')]
    unnamed x8 -> x10, local copies, waits for them, and re-layouts: 2 us -> 11.9 us
    reduce_sum x0 -> x1, other arithmetic: none -> 1.91 us  [body(): jnp.sum(lax.all_gather(jnp.concatenate([out_part, in_part], axis=1), 'ten...]
where the time goes in v1:
time: 121 us
  waiting for transfers between devices  58.9 us (49%)
  blocking collectives  23.7 us (20%)
  between operations  14.1 us (12%)
  local copies, waits for them, and re-layouts  12.8 us (11%)
  matrix products  8.58 us (7%)
  other arithmetic  2.89 us (2%)
    all_gather x1, waiting for transfers between devices, body(): lax.all_gather(jnp.concatenate([out_part, in_part], axis=1), 'tensor')  58.9 us
    all_gather x1, blocking collectives, body(): piece = lax.all_gather(full_blocks, 'dp', axis=0, tiled=True)  23.7 us
    unnamed x10, local copies, waits for them, and re-layouts  11.9 us
    dot_general x1, matrix products, body(): out_part = jnp.dot(grad_rows, proj_out, preferred_element_type=jnp.float32)  5.24 us
  transfers between devices with their start and end apart: 1, of which 1 were waited for; matrix products, arithmetic and copies ran while one was open for 0% of the time, Pallas kernels for 0%

profile of v1, /device:TPU:2, one launch (start us, length us, event | category | flops | bytes accessed | tf_op | source)
XLA Modules:
  0.0 121.1 jit_solution(15396115744396495787)
XLA Ops:
  7.2 0.0 copy-start
  7.2 0.0 copy-start.1
  7.2 0.0 all-gather.4.cloned.1.call-start
  7.2 1.5 %copy-done = bf16[2,512,1024]{2,1,0:T(8,128)(2,1)S(1)} copy-done((bf16[2,512,1024]{2,1,0:T(8,128)(2,1)S(1)}, bf16[2,512,1024]{2,1,0:T(8,128)(2,1)}, u32[]{:S(2)}) %copy-start) | copy-done | bytes 2097176
  8.8 1.7 %fusion.7 = f32[1024,64]{0,1:T(8,128)S(1)} fusion(bf16[1024,1024]{1,0:T(8,128)(2,1)S(1)} %bitcast.23, bf16[1024,64]{0,1:T(8,128)(2,1)} %param.8), kind=kOutput, calls=%fused_computation.15 | convolution fusion | flops 134217728 | bytes 2490368 | tf_op jit(solution)/shard_map/dot_general | solution.py:19
  10.4 5.2 %fusion.6 = f32[1024,64]{0,1:T(8,128)S(1)} fusion(bf16[1024,3328]{1,0:T(8,128)(2,1)} %bitcast.24, bf16[3328,64]{0,1:T(8,128)(2,1)} %param.9), kind=kOutput, calls=%fused_computation.14 | convolution fusion | flops 436207616 | bytes 7503872 | tf_op jit(solution)/shard_map/dot_general | solution.py:18
  15.7 0.9 pad_maximum_fusion
  16.6 0.0 all-gather.4.cloned.1.call-update
  16.6 0.0 copy-done.1
  16.6 0.1 compare_convert_fusion
  16.7 58.9 %all-gather.4.cloned.1.call-done = f32[16384,128]{0,1:T(8,128)} async-done(((f32[1024,128]{0,1:T(8,128)}), f32[16384,128]{0,1:T(8,128)}) %all-gather.4.cloned.1.call-update) | async-done | bytes 8388624 | tf_op jit(solution)/shard_map/all_gather | solution.py:20
  75.6 9.9 %copy.13 = f32[16,8,16,1024]{3,2,1,0:T(8,128)S(1)} copy(f32[16,8,16,1024]{3,1,2,0:T(8,128)} %bitcast.25) | data formatting | bytes 16777216
  85.5 0.0 copy-start.2
  85.5 1.9 %bitcast_reduce_fusion = f32[1024,128]{0,1:T(8,128)S(1)} fusion(f32[16,8,16,1024]{3,2,1,0:T(8,128)S(1)} %copy.13), kind=kLoop, calls=%fused_computation | loop fusion | flops 1966080 | bytes 8912896 | tf_op jit(solution)/shard_map/reduce_sum | solution.py:20
  87.4 0.2 reshape.44
  87.7 0.4 convolution_multiply_fusion
  88.1 0.1 reshape.46
  88.2 0.1 reshape.48
  88.3 23.7 %all-gather.1 = f32[16,2,4096]{2,1,0:T(2,128)S(1)} all-gather(f32[1,2,4096]{2,1,0:T(2,128)S(1)} %reshape.48), channel_id=1, replica_groups=mesh['dp'=16,'tensor'=16] {'dp'}, dimensions={0}, use_global_device_ids=true | all-gather | bytes 557056 | tf_op jit(solution)/shard_map/all_gather | solution.py:29
  112.0 0.4 reshape.49
  112.4 0.6 constant_dynamic-slice_fusion
  113.0 0.0 copy-done.2
  113.0 0.3 fusion.3
  113.3 1.0 convolution_multiply_fusion.1
  (3 shorter events, 0.1 us)
Async XLA Ops:
  7.2 1.6 %copy-start = (bf16[2,512,1024]{2,1,0:T(8,128)(2,1)S(1)}, bf16[2,512,1024]{2,1,0:T(8,128)(2,1)}, u32[]{:S(2)}) copy-start(bf16[2,512,1024]{2,1,0:T(8,128)(2,1)} %param.6) | copy-start | bytes 6291460
  7.2 9.4 %copy-start.1 = (s32[2]{0:T(128)S(1)}, s32[2]{0:T(128)}, u32[]{:S(2)}) copy-start(s32[2]{0:T(128)} %param.10) | copy-start | bytes 28
  7.2 68.4 %all-gather.4.cloned.1.call-start = ((), (), s32[]{:S(2)}) async-start(), calls=%async_computation | async-start | bytes 8912896 | tf_op jit(solution)/shard_map/all_gather | solution.py:20
  85.5 27.5 %copy-start.2 = (s32[16]{0:T(128)S(1)}, s32[16]{0:T(128)}, u32[]{:S(2)}) copy-start(s32[16]{0:T(128)} %param.11) | copy-start | bytes 196
Sparse Core Ops, SparseCore 0:
  16.7 58.8 all-gather.3
